TPU v7x, 256 devices: a whole 4x4x8 slice. The times are simulated.
256 devices in a mesh: replica: 32 (over x, z_hi, core), fsdp: 8 (over y, z_lo).
Axes of the slice: x: 4, y: 4, z: 8 (z_hi: 4, z_lo: 2; z = z_hi * 2 + z_lo), core: 2. Of those that a mesh axis runs over, the one named last changes fastest.
Arguments:
- tokens: bfloat16 [65536, 8192], P(('replica', 'fsdp')), may hold values from -6 to 6
- cotangent: bfloat16 [65536, 512], P(('replica', 'fsdp')), may hold values from -0.125 to 0.125
- gain: float32 [32, 8192], P('replica'), may hold values from 0.1 to 1.9
- value_weight: bfloat16 [32, 8192, 512], P('replica', 'fsdp'), may hold values from -0.25 to 0.25
- fragment: bfloat16 [32, 8192, 1024], P('replica', 'fsdp'), may hold values from -6 to 6
- global_table: float32 [4, 8192, 1024], P(None, ('fsdp', 'replica')), may hold values from -6 to 6
- momentum_table: float32 [4, 8192, 1024], P(None, ('fsdp', 'replica')), may hold values from -4 to 4
- frag_index: int32 [], replicated, may hold values from 0 to 3
Outputs:
- weight_grad: bfloat16 [32, 8192, 512], P('replica', 'fsdp')
- gain_grad: float32 [32, 8192], P('replica')
- new_fragment: bfloat16 [32, 8192, 1024], P('replica', 'fsdp')
- new_global: float32 [4, 8192, 1024], P(None, ('fsdp', 'replica'))
- new_momentum: float32 [4, 8192, 1024], P(None, ('fsdp', 'replica'))
All inputs are finite; a program needn't handle non-finite values.
Results may differ from a plain program's by a relative error of at most 0.017.
Values may be sent and summed in bfloat16 or wider, within the bound.
A program may use at most 128 MiB of HBM per device.

v0:
```python
import jax
import jax.numpy as jnp
from jax import lax
from jax.sharding import PartitionSpec as P

epsilon = 1e-05
outer_rate = 0.7
outer_beta = 0.9
mix_weight = 0.5


def body(tokens, cotangent, gain, value_weight, fragment, global_table, momentum_table, frag_index):
    gains = gain[0]
    weight = value_weight[0]
    floats = tokens.astype(jnp.float32)
    inverse = lax.rsqrt(jnp.mean(floats * floats, axis=-1, keepdims=True) + epsilon)
    normed = floats * inverse
    scaled = (normed * gains).astype(jnp.bfloat16)
    back = lax.dot_general(
        cotangent,
        lax.all_gather(weight, "fsdp", axis=0, tiled=True),
        (((1,), (1,)), ((), ())),
        preferred_element_type=jnp.float32,
    )
    columns = normed
    partial_gain = jnp.sum(columns * back, axis=0)
    gain_grad = lax.psum(partial_gain, "fsdp")
    columns = scaled
    weight_grad = lax.psum_scatter(
        lax.dot_general(
            columns, cotangent, (((0,), (0,)), ((), ())), preferred_element_type=jnp.float32
        ).astype(jnp.bfloat16),
        "fsdp",
        scatter_dimension=0,
        tiled=True,
    )
    chosen = lax.dynamic_index_in_dim(global_table, frag_index, 0, keepdims=False)
    velocity = lax.dynamic_index_in_dim(momentum_table, frag_index, 0, keepdims=False)
    local = fragment[0].astype(jnp.float32)
    replicas = lax.axis_size("replica")
    summed = lax.psum_scatter(
        local.astype(jnp.bfloat16), "replica", scatter_dimension=0, tiled=True
    ).astype(jnp.float32)
    delta = chosen - summed / replicas
    new_velocity = outer_beta * velocity + delta
    new_params = chosen - outer_rate * (delta + outer_beta * new_velocity)
    full_params = lax.all_gather(new_params, "replica", axis=0, tiled=True)
    new_fragment = (mix_weight * local + (1.0 - mix_weight) * full_params).astype(jnp.bfloat16)[
        None
    ]
    new_global = lax.dynamic_update_index_in_dim(global_table, new_params, frag_index, 0)
    new_momentum = lax.dynamic_update_index_in_dim(momentum_table, new_velocity, frag_index, 0)
    return (weight_grad[None], gain_grad[None], new_fragment, new_global, new_momentum)


def solution(mesh):
    placed = (
        P(("replica", "fsdp"), None),
        P(("replica", "fsdp"), None),
        P("replica", None),
        P("replica", "fsdp", None),
        P("replica", "fsdp", None),
        P(None, ("fsdp", "replica"), None),
        P(None, ("fsdp", "replica"), None),
        P(),
    )
    return jax.shard_map(
        body,
        mesh=mesh,
        in_specs=placed,
        out_specs=(
            P("replica", "fsdp", None),
            P("replica", None),
            P("replica", "fsdp", None),
            P(None, ("fsdp", "replica"), None),
            P(None, ("fsdp", "replica"), None),
        ),
        check_vma=False,
    )
```

profile of v0, /device:TPU:1, one launch (start us, length us, event | category | flops | bytes accessed | tf_op | source)
XLA Modules:
  0.0 521.8 jit_solution(3852087064441866261)
XLA Ops:
  7.2 0.0 copy-start
  7.2 0.0 copy-start.5
  7.2 0.0 reduce-scatter.5.cloned.1.call-start
  7.2 1.1 copy.18
  8.3 1.0 copy.19
  9.4 0.0 reduce-scatter.5.cloned.1.call-update
  9.4 0.0 all-gather.4.cloned.1.call-start
  10.1 95.1 %reduce-scatter.5.cloned.1.call-done = bf16[32,1024]{1,0:T(8,128)(2,1)} async-done(((bf16[1024,1024]{1,0:T(8,128)(2,1)}), bf16[32,1024]{1,0:T(8,128)(2,1)}) %reduce-scatter.5.cloned.1.call-update) | async-done | bytes 65552 | tf_op jit(solution)/shard_map/reduce_scatter | solution.py:41
  105.2 1.6 bitcast_subtract_fusion
  106.8 0.0 all-gather.4.cloned.1.call-update
  106.8 0.0 all-gather.6.cloned.1.call-start
  106.9 0.7 all-gather.6.cloned.1.call-update
  107.5 0.0 reduce-scatter.3.cloned.1.call-start
  107.6 3.1 fusion.2
  110.7 0.0 copy-done
  110.7 0.0 copy-done.5
  110.7 8.1 %convolution_convert_fusion = bf16[8192,512]{1,0:T(8,128)(2,1)} fusion(bf16[256,512]{1,0:T(8,128)(2,1)S(1)} %copy-done, bf16[256,8192]{1,0:T(8,128)(2,1)} %param.8, f32[8192]{0:T(1024)S(1)} %bitcast.32, f32[256]{0:T(256)S(1)} %add_rsqrt_fusion), kind=kOutput, calls=%fused_computation | convolution fusion | flops 2160066560 | bytes 12878848 | tf_op jit(solution)/shard_map/dot_general | solution.py:30
  118.9 0.0 copy-start.2
  118.9 0.0 copy-start.1
  118.9 0.0 reduce-scatter.3.cloned.1.call-update
  118.9 0.9 copy-done.2
  119.8 0.9 bitcast_dynamic-update-slice_fusion
  120.7 0.0 copy-start.3
  120.7 0.0 copy-start.4
  120.7 48.0 %all-gather.4.cloned.1.call-done = f32[1024,1024]{1,0:T(8,128)} async-done(((f32[32,1024]{1,0:T(8,128)}), f32[1024,1024]{1,0:T(8,128)}) %all-gather.4.cloned.1.call-update) | async-done | bytes 4194320 | tf_op jit(solution)/shard_map/all_gather | solution.py:47
  168.8 0.0 copy-done.1
  168.8 4.3 fusion.7
  173.1 165.6 %all-gather.6.cloned.1.call-done = bf16[1,8192,512]{2,1,0:T(8,128)(2,1)} async-done(((bf16[1,1024,512]{2,1,0:T(8,128)(2,1)}), bf16[1,8192,512]{2,1,0:T(8,128)(2,1)}) %all-gather.6.cloned.1.call-update) | async-done | bytes 8388624 | tf_op jit(solution)/shard_map/all_gather | solution.py:21
  338.6 7.0 %fusion.8 = f32[8192]{0:T(1024)S(1)} fusion(bf16[256,512]{1,0:T(8,128)(2,1)S(1)} %copy-done, bf16[1,8192,512]{2,1,0:T(8,128)(2,1)} %all-gather.6.cloned.1.call-done, f32[256]{0:T(256)S(1)} %add_rsqrt_fusion, bf16[256,8192]{1,0:T(8,128)(2,1)} %param.8), kind=kOutput, calls=%fused_computation.12 | convolution fusion | flops 2155864064 | bytes 12878848 | tf_op jit(solution)/shard_map/dot_general | solution.py:19
  345.6 0.0 copy-done.3
  345.6 0.0 copy-done.4
  345.6 27.4 %psum.7 = f32[1,8192]{1,0:T(1,128)} all-reduce(f32[1,8192]{1,0:T(1,128)S(1)} %bitcast.30), channel_id=1, replica_groups=mesh['replica'=32,'fsdp'=8] {'fsdp'}, use_global_device_ids=true, to_apply=%region_3.0 | all-reduce | flops 8192 | bytes 65536 | tf_op jit(solution)/shard_map/psum | solution.py:27
  373.0 142.2 %reduce-scatter.3.cloned.1.call-done = bf16[1024,512]{1,0:T(8,128)(2,1)} async-done(((bf16[8192,512]{1,0:T(8,128)(2,1)}), bf16[1024,512]{1,0:T(8,128)(2,1)}) %reduce-scatter.3.cloned.1.call-update) | async-done | bytes 1048592 | tf_op jit(solution)/shard_map/reduce_scatter | solution.py:29
  (1 shorter events, 0.0 us)
Async XLA Ops:
  7.2 103.5 %copy-start = (bf16[256,512]{1,0:T(8,128)(2,1)S(1)}, bf16[256,512]{1,0:T(8,128)(2,1)}, u32[]{:S(2)}) copy-start(bf16[256,512]{1,0:T(8,128)(2,1)} %param.9) | copy-start | bytes 786436
  7.2 103.5 %copy-start.5 = (f32[1,8192]{1,0:T(1,128)S(1)}, f32[1,8192]{1,0:T(1,128)}, u32[]{:S(2)}) copy-start(f32[1,8192]{1,0:T(1,128)} %param.10) | copy-start | bytes 98308
  7.2 98.0 %reduce-scatter.5.cloned.1.call-start = ((), (), s32[]{:S(2)}) async-start(), calls=%async_computation.3 | async-start | bytes 2162688 | tf_op jit(solution)/shard_map/reduce_scatter | solution.py:41
  9.4 159.4 %all-gather.4.cloned.1.call-start = ((), (), s32[]{:S(2)}) async-start(), calls=%async_computation.4 | async-start | bytes 4325376 | tf_op jit(solution)/shard_map/all_gather | solution.py:47
  106.8 231.8 %all-gather.6.cloned.1.call-start = ((), (), s32[]{:S(2)}) async-start(), calls=%async_computation.5 | async-start | bytes 9437184 | tf_op jit(solution)/shard_map/all_gather | solution.py:21
  107.5 407.7 %reduce-scatter.3.cloned.1.call-start = ((), (), s32[]{:S(2)}) async-start(), calls=%async_computation.2 | async-start | bytes 9437184 | tf_op jit(solution)/shard_map/reduce_scatter | solution.py:29
  118.9 0.9 copy-start.2
  118.9 49.9 %copy-start.1 = (bf16[1,1024,1024]{2,1,0:T(8,128)(2,1)S(1)}, bf16[1,1024,1024]{2,1,0:T(8,128)(2,1)}, u32[]{:S(2)}) copy-start(bf16[1,1024,1024]{2,1,0:T(8,128)(2,1)} %param.12) | copy-start | bytes 6291460
  120.7 224.9 %copy-start.3 = (f32[4,32,1024]{2,1,0:T(8,128)}, f32[4,32,1024]{2,1,0:T(8,128)S(1)}, u32[]{:S(2)}) copy-start(f32[4,32,1024]{2,1,0:T(8,128)S(1)} %get-tuple-element.8) | copy-start | bytes 1572868
  120.7 224.9 %copy-start.4 = (f32[4,32,1024]{2,1,0:T(8,128)}, f32[4,32,1024]{2,1,0:T(8,128)S(1)}, u32[]{:S(2)}) copy-start(f32[4,32,1024]{2,1,0:T(8,128)S(1)} %get-tuple-element.7) | copy-start | bytes 1572868
Sparse Core Ops, SparseCore 0:
  11.9 93.3 reduce-scatter.4
  108.3 60.3 all-gather.3
  170.6 167.9 all-gather.5
  341.6 173.5 reduce-scatter.2
where the time goes:
time: 522 us
  waiting for transfers between devices  452 us (87%)
  blocking collectives  27.4 us (5%)
  matrix products  15.1 us (3%)
  between operations  14.5 us (3%)
  other arithmetic  8.97 us (2%)
    all_gather x1, waiting for transfers between devices, body(): lax.all_gather(weight, 'fsdp', axis=0, tiled=True)  166 us
    reduce_scatter x1, waiting for transfers between devices, body(): lax.psum_scatter(lax.dot_general(columns, cotangent, (((0,), (0,)), ((),...  142 us
    reduce_scatter x1, waiting for transfers between devices, body(): lax.psum_scatter(local.astype(jnp.bfloat16), 'replica', scatter_dimension...  95.1 us
    all_gather x1, waiting for transfers between devices, body(): full_params = lax.all_gather(new_params, 'replica', axis=0, tiled=True)  48 us
    psum x1, blocking collectives, body(): gain_grad = lax.psum(partial_gain, 'fsdp')  27.4 us
  transfers between devices with their start and end apart: 4, of which 4 were waited for; matrix products, arithmetic and copies ran while one was open for 4% of the time, Pallas kernels for 0%

commit v1 on v0

--- a/solution.py
+++ b/solution.py
@@ -24,7 +24,7 @@
     )
     columns = normed
     partial_gain = jnp.sum(columns * back, axis=0)
-    gain_grad = lax.psum(partial_gain, "fsdp")
+    gain_grad = jnp.sum(lax.all_gather(partial_gain, "fsdp"), axis=0)
     columns = scaled
     weight_grad = lax.psum_scatter(
         lax.dot_general(

time: 522 us -> 524 us (level)
    psum x1 -> x0, blocking collectives: 27.4 us -> none  [body(): gain_grad = lax.psum(partial_gain, 'fsdp')]
    all_gather x0 -> x1, blocking collectives: none -> 24.1 us  [body(): gain_grad = jnp.sum(lax.all_gather(partial_gain, 'fsdp'), axis=0)]
  transfers between devices with their start and end apart: 4 -> 4, of which waited for: 4 -> 4; matrix products, arithmetic and copies ran while one was open for 4% -> 5% of each run, Pallas kernels for 0% -> 0%
where the time goes in v1:
time: 524 us
  waiting for transfers between devices  457 us (87%)
  blocking collectives  24.1 us (5%)
  matrix products  15.1 us (3%)
  between operations  14.5 us (3%)
  other arithmetic  9.65 us (2%)
    all_gather x1, waiting for transfers between devices, body(): lax.all_gather(weight, 'fsdp', axis=0, tiled=True)  166 us
    reduce_scatter x1, waiting for transfers between devices, body(): lax.psum_scatter(lax.dot_general(columns, cotangent, (((0,), (0,)), ((),...  147 us
    reduce_scatter x1, waiting for transfers between devices, body(): lax.psum_scatter(local.astype(jnp.bfloat16), 'replica', scatter_dimension...  95.1 us
    all_gather x1, waiting for transfers between devices, body(): full_params = lax.all_gather(new_params, 'replica', axis=0, tiled=True)  48 us
    all_gather x1, blocking collectives, body(): gain_grad = jnp.sum(lax.all_gather(partial_gain, 'fsdp'), axis=0)  24.1 us
  transfers between devices with their start and end apart: 4, of which 4 were waited for; matrix products, arithmetic and copies ran while one was open for 5% of the time, Pallas kernels for 0%

profile of v1, /device:TPU:1, one launch (start us, length us, event | category | flops | bytes accessed | tf_op | source)
XLA Modules:
  0.0 524.1 jit_solution(11299679481191658599)
XLA Ops:
  7.2 0.0 copy-start
  7.2 0.0 copy-start.5
  7.2 0.0 reduce-scatter.5.cloned.1.call-start
  7.2 1.1 copy.18
  8.3 1.0 copy.19
  9.4 0.0 reduce-scatter.5.cloned.1.call-update
  9.4 0.0 all-gather.5.cloned.1.call-start
  10.1 95.1 %reduce-scatter.5.cloned.1.call-done = bf16[32,1024]{1,0:T(8,128)(2,1)} async-done(((bf16[1024,1024]{1,0:T(8,128)(2,1)}), bf16[32,1024]{1,0:T(8,128)(2,1)}) %reduce-scatter.5.cloned.1.call-update) | async-done | bytes 65552 | tf_op jit(solution)/shard_map/reduce_scatter | solution.py:41
  105.2 1.6 bitcast_subtract_fusion
  106.8 0.0 all-gather.5.cloned.1.call-update
  106.8 0.0 all-gather.7.cloned.1.call-start
  106.9 0.7 all-gather.7.cloned.1.call-update
  107.5 0.0 reduce-scatter.3.cloned.1.call-start
  107.6 3.1 fusion.2
  110.7 0.0 copy-done
  110.7 0.0 copy-done.5
  110.7 8.1 %convolution_convert_fusion = bf16[8192,512]{1,0:T(8,128)(2,1)} fusion(bf16[256,512]{1,0:T(8,128)(2,1)S(1)} %copy-done, bf16[256,8192]{1,0:T(8,128)(2,1)} %param.8, f32[8192]{0:T(1024)S(1)} %bitcast.32, f32[256]{0:T(256)S(1)} %add_rsqrt_fusion), kind=kOutput, calls=%fused_computation | convolution fusion | flops 2160066560 | bytes 12878848 | tf_op jit(solution)/shard_map/dot_general | solution.py:30
  118.9 0.0 copy-start.2
  118.9 0.0 copy-start.1
  118.9 0.0 reduce-scatter.3.cloned.1.call-update
  118.9 0.9 copy-done.2
  119.8 0.9 bitcast_dynamic-update-slice_fusion
  120.7 0.0 copy-start.3
  120.7 0.0 copy-start.4
  120.7 48.0 %all-gather.5.cloned.1.call-done = f32[1024,1024]{1,0:T(8,128)} async-done(((f32[32,1024]{1,0:T(8,128)}), f32[1024,1024]{1,0:T(8,128)}) %all-gather.5.cloned.1.call-update) | async-done | bytes 4194320 | tf_op jit(solution)/shard_map/all_gather | solution.py:47
  168.8 0.0 copy-done.1
  168.8 4.3 fusion.7
  173.1 165.6 %all-gather.7.cloned.1.call-done = bf16[1,8192,512]{2,1,0:T(8,128)(2,1)} async-done(((bf16[1,1024,512]{2,1,0:T(8,128)(2,1)}), bf16[1,8192,512]{2,1,0:T(8,128)(2,1)}) %all-gather.7.cloned.1.call-update) | async-done | bytes 8388624 | tf_op jit(solution)/shard_map/all_gather | solution.py:21
  338.6 7.0 %fusion.8 = f32[8192]{0:T(1024)S(1)} fusion(bf16[256,512]{1,0:T(8,128)(2,1)S(1)} %copy-done, bf16[1,8192,512]{2,1,0:T(8,128)(2,1)} %all-gather.7.cloned.1.call-done, f32[256]{0:T(256)S(1)} %add_rsqrt_fusion, bf16[256,8192]{1,0:T(8,128)(2,1)} %param.8), kind=kOutput, calls=%fused_computation.12 | convolution fusion | flops 2155864064 | bytes 12878848 | tf_op jit(solution)/shard_map/dot_general | solution.py:19
  345.6 0.0 copy-done.3
  345.6 0.0 copy-done.4
  345.6 24.1 %all-gather.1 = f32[65536]{0:T(1024)S(1)} all-gather(f32[8192]{0:T(1024)S(1)} %fusion.8), channel_id=3, replica_groups=mesh['replica'=32,'fsdp'=8] {'fsdp'}, dimensions={0}, use_global_device_ids=true | all-gather | bytes 294912 | tf_op jit(solution)/shard_map/all_gather | solution.py:27
  369.7 0.1 reshape.21
  369.7 0.7 reduce_sum.29
  370.4 147.1 %reduce-scatter.3.cloned.1.call-done = bf16[1024,512]{1,0:T(8,128)(2,1)} async-done(((bf16[8192,512]{1,0:T(8,128)(2,1)}), bf16[1024,512]{1,0:T(8,128)(2,1)}) %reduce-scatter.3.cloned.1.call-update) | async-done | bytes 1048592 | tf_op jit(solution)/shard_map/reduce_scatter | solution.py:29
  (1 shorter events, 0.0 us)
Async XLA Ops:
  7.2 103.5 %copy-start = (bf16[256,512]{1,0:T(8,128)(2,1)S(1)}, bf16[256,512]{1,0:T(8,128)(2,1)}, u32[]{:S(2)}) copy-start(bf16[256,512]{1,0:T(8,128)(2,1)} %param.9) | copy-start | bytes 786436
  7.2 103.5 %copy-start.5 = (f32[1,8192]{1,0:T(1,128)S(1)}, f32[1,8192]{1,0:T(1,128)}, u32[]{:S(2)}) copy-start(f32[1,8192]{1,0:T(1,128)} %param.10) | copy-start | bytes 98308
  7.2 98.0 %reduce-scatter.5.cloned.1.call-start = ((), (), s32[]{:S(2)}) async-start(), calls=%async_computation.3 | async-start | bytes 2162688 | tf_op jit(solution)/shard_map/reduce_scatter | solution.py:41
  9.4 159.4 %all-gather.5.cloned.1.call-start = ((), (), s32[]{:S(2)}) async-start(), calls=%async_computation.4 | async-start | bytes 4325376 | tf_op jit(solution)/shard_map/all_gather | solution.py:47
  106.8 231.8 %all-gather.7.cloned.1.call-start = ((), (), s32[]{:S(2)}) async-start(), calls=%async_computation.5 | async-start | bytes 9437184 | tf_op jit(solution)/shard_map/all_gather | solution.py:21
  107.5 410.0 %reduce-scatter.3.cloned.1.call-start = ((), (), s32[]{:S(2)}) async-start(), calls=%async_computation.2 | async-start | bytes 9437184 | tf_op jit(solution)/shard_map/reduce_scatter | solution.py:29
  118.9 0.9 copy-start.2
  118.9 49.9 %copy-start.1 = (bf16[1,1024,1024]{2,1,0:T(8,128)(2,1)S(1)}, bf16[1,1024,1024]{2,1,0:T(8,128)(2,1)}, u32[]{:S(2)}) copy-start(bf16[1,1024,1024]{2,1,0:T(8,128)(2,1)} %param.12) | copy-start | bytes 6291460
  120.7 224.9 %copy-start.3 = (f32[4,32,1024]{2,1,0:T(8,128)}, f32[4,32,1024]{2,1,0:T(8,128)S(1)}, u32[]{:S(2)}) copy-start(f32[4,32,1024]{2,1,0:T(8,128)S(1)} %get-tuple-element.8) | copy-start | bytes 1572868
  120.7 224.9 %copy-start.4 = (f32[4,32,1024]{2,1,0:T(8,128)}, f32[4,32,1024]{2,1,0:T(8,128)S(1)}, u32[]{:S(2)}) copy-start(f32[4,32,1024]{2,1,0:T(8,128)S(1)} %get-tuple-element.7) | copy-start | bytes 1572868
Sparse Core Ops, SparseCore 0:
  11.9 93.3 reduce-scatter.4
  108.3 60.3 all-gather.4
  170.6 167.9 all-gather.6
  341.6 175.9 reduce-scatter.2

commit v2 on v0

--- a/solution.py
+++ b/solution.py
@@ -18,7 +18,9 @@
     scaled = (normed * gains).astype(jnp.bfloat16)
     back = lax.dot_general(
         cotangent,
-        lax.all_gather(weight, "fsdp", axis=0, tiled=True),
+        jnp.concatenate(
+            lax.all_to_all(jnp.stack([weight] * lax.axis_size("fsdp")), "fsdp", 0, 0), axis=0
+        ),
         (((1,), (1,)), ((), ())),
         preferred_element_type=jnp.float32,
     )

time: 522 us -> 408 us (0.78)
  waiting for transfers between devices: 452 us -> 318 us
  blocking collectives: 27.4 us -> 35.9 us
    all_gather x1 -> x0, waiting for transfers between devices: 166 us -> none  [body(): lax.all_gather(weight, 'fsdp', axis=0, tiled=True)]
    all_gather x1, waiting for transfers between devices: 48 us -> 203 us  [body(): full_params = lax.all_gather(new_params, 'replica', axis=0, tiled=True)]
    reduce_scatter x1, waiting for transfers between devices: 142 us -> 19.2 us  [body(): lax.psum_scatter(lax.dot_general(columns, cotangent, (((0,), (0,)), ((),...]
    psum x1, blocking collectives: 27.4 us -> 35.9 us  [body(): gain_grad = lax.psum(partial_gain, 'fsdp')]
  transfers between devices with their start and end apart: 4 -> 4, of which waited for: 4 -> 3; matrix products, arithmetic and copies ran while one was open for 4% -> 7% of each run, Pallas kernels for 0% -> 0%
where the time goes in v2:
time: 408 us
  waiting for transfers between devices  318 us (78%)
  blocking collectives  35.9 us (9%)
  between operations  16.2 us (4%)
  matrix products  15.2 us (4%)
  other arithmetic  8.97 us (2%)
  local copies, waits for them, and re-layouts  8.27 us (2%)
  starting transfers between devices  5.26 us (1%)
    all_gather x1, waiting for transfers between devices, body(): full_params = lax.all_gather(new_params, 'replica', axis=0, tiled=True)  203 us
    reduce_scatter x1, waiting for transfers between devices, body(): lax.psum_scatter(local.astype(jnp.bfloat16), 'replica', scatter_dimension...  95.1 us
    psum x1, blocking collectives, body(): gain_grad = lax.psum(partial_gain, 'fsdp')  35.9 us
    reduce_scatter x1, waiting for transfers between devices, body(): lax.psum_scatter(lax.dot_general(columns, cotangent, (((0,), (0,)), ((),...  19.2 us
    dot_general x1, matrix products, body(): lax.dot_general(columns, cotangent, (((0,), (0,)), ((), ())), preferred_e...  8.17 us
  transfers between devices with their start and end apart: 4, of which 3 were waited for; matrix products, arithmetic and copies ran while one was open for 7% of the time, Pallas kernels for 0%

profile of v2, /device:TPU:1, one launch (start us, length us, event | category | flops | bytes accessed | tf_op | source)
XLA Modules:
  0.0 407.7 jit_solution(17397073163510286047)
XLA Ops:
  8.0 0.0 copy-start
  8.0 0.0 copy-start.6
  8.0 0.0 reduce-scatter.5.cloned.1.call-start
  8.1 1.1 copy.18
  9.1 1.0 copy.19
  10.2 0.0 reduce-scatter.5.cloned.1.call-update
  10.2 0.0 all-gather.2.cloned.1.call-start
  10.9 95.1 %reduce-scatter.5.cloned.1.call-done = bf16[32,1024]{1,0:T(8,128)(2,1)} async-done(((bf16[1024,1024]{1,0:T(8,128)(2,1)}), bf16[32,1024]{1,0:T(8,128)(2,1)}) %reduce-scatter.5.cloned.1.call-update) | async-done | bytes 65552 | tf_op jit(solution)/shard_map/reduce_scatter | solution.py:43
  106.0 1.6 bitcast_subtract_fusion
  107.6 0.0 all-gather.2.cloned.1.call-update
  107.6 0.0 reduce-scatter.3.cloned.1.call-start
  107.7 3.1 fusion.2
  110.8 0.0 copy-done
  110.8 0.0 copy-done.6
  110.8 8.2 %convolution_convert_fusion = bf16[8192,512]{1,0:T(8,128)(2,1)} fusion(bf16[256,512]{1,0:T(8,128)(2,1)S(1)} %copy-done, bf16[256,8192]{1,0:T(8,128)(2,1)} %param.8, f32[8192]{0:T(1024)S(1)} %bitcast.31, f32[256]{0:T(256)S(1)} %add_rsqrt_fusion), kind=kOutput, calls=%fused_computation | convolution fusion | flops 2160066560 | bytes 12878848 | tf_op jit(solution)/shard_map/dot_general | solution.py:32
  119.0 0.0 copy-start.3
  119.0 0.0 reduce-scatter.3.cloned.1.call-update
  119.0 1.2 copy-done.3
  120.2 3.9 stack.3
  124.2 0.0 copy-start.2
  124.2 0.0 copy-start.1
  124.2 5.1 %all-to-all-start = ((bf16[8,1024,512]{2,1,0:T(8,128)(2,1)}), bf16[8,1024,512]{2,1,0:T(8,128)(2,1)}, u32[]{:S(2)}, u32[]{:S(2)}) async-start(bf16[8,1024,512]{2,1,0:T(8,128)(2,1)} %stack.3), calls=%async_computation.1 | async-start | bytes 16777216 | tf_op jit(solution)/shard_map/all_to_all | solution.py:22
  129.3 0.0 copy-done.2
  129.3 1.0 bitcast_dynamic-update-slice_fusion
  130.3 0.0 copy-start.4
  130.3 0.0 copy-start.5
  130.3 203.4 %all-gather.2.cloned.1.call-done = f32[1024,1024]{1,0:T(8,128)} async-done(((f32[32,1024]{1,0:T(8,128)}), f32[1024,1024]{1,0:T(8,128)}) %all-gather.2.cloned.1.call-update) | async-done | bytes 4194320 | tf_op jit(solution)/shard_map/all_gather | solution.py:49
  333.8 0.0 copy-done.1
  333.8 4.3 %fusion.6 = bf16[1,1024,1024]{2,1,0:T(8,128)(2,1)} fusion(f32[1024,1024]{1,0:T(8,128)} %all-gather.2.cloned.1.call-done, bf16[1,1024,1024]{2,1,0:T(8,128)(2,1)S(1)} %copy-done.1), kind=kLoop, calls=%fused_computation.10 | loop fusion | flops 4194304 | bytes 8388608 | tf_op jit(solution)/shard_map/broadcast_in_dim | solution.py:50
  338.0 0.0 all-to-all-done
  338.0 7.1 %fusion.7 = f32[8192]{0:T(1024)S(1)} fusion(bf16[256,512]{1,0:T(8,128)(2,1)S(1)} %copy-done, bf16[8192,512]{1,0:T(8,128)(2,1)} %bitcast.3, f32[256]{0:T(256)S(1)} %add_rsqrt_fusion, bf16[256,8192]{1,0:T(8,128)(2,1)} %param.8), kind=kOutput, calls=%fused_computation.11 | convolution fusion | flops 2155864064 | bytes 12878848 | tf_op jit(solution)/shard_map/dot_general | solution.py:19
  345.1 0.0 copy-done.4
  345.1 0.0 copy-done.5
  345.1 35.9 %psum.7 = f32[1,8192]{1,0:T(1,128)} all-reduce(f32[1,8192]{1,0:T(1,128)S(1)} %bitcast.29), channel_id=1, replica_groups=mesh['replica'=32,'fsdp'=8] {'fsdp'}, use_global_device_ids=true, to_apply=%region_3.0 | all-reduce | flops 8192 | bytes 65536 | tf_op jit(solution)/shard_map/psum | solution.py:29
  381.0 19.2 %reduce-scatter.3.cloned.1.call-done = bf16[1024,512]{1,0:T(8,128)(2,1)} async-done(((bf16[8192,512]{1,0:T(8,128)(2,1)}), bf16[1024,512]{1,0:T(8,128)(2,1)}) %reduce-scatter.3.cloned.1.call-update) | async-done | bytes 1048592 | tf_op jit(solution)/shard_map/reduce_scatter | solution.py:31
  (1 shorter events, 0.0 us)
Async XLA Ops:
  8.0 102.8 %copy-start = (bf16[256,512]{1,0:T(8,128)(2,1)S(1)}, bf16[256,512]{1,0:T(8,128)(2,1)}, u32[]{:S(2)}) copy-start(bf16[256,512]{1,0:T(8,128)(2,1)} %param.9) | copy-start | bytes 786436
  8.0 102.8 %copy-start.6 = (f32[1,8192]{1,0:T(1,128)S(1)}, f32[1,8192]{1,0:T(1,128)}, u32[]{:S(2)}) copy-start(f32[1,8192]{1,0:T(1,128)} %param.10) | copy-start | bytes 98308
  8.0 98.0 %reduce-scatter.5.cloned.1.call-start = ((), (), s32[]{:S(2)}) async-start(), calls=%async_computation.4 | async-start | bytes 2162688 | tf_op jit(solution)/shard_map/reduce_scatter | solution.py:43
  10.2 323.5 %all-gather.2.cloned.1.call-start = ((), (), s32[]{:S(2)}) async-start(), calls=%async_computation.5 | async-start | bytes 4325376 | tf_op jit(solution)/shard_map/all_gather | solution.py:49
  107.6 292.6 %reduce-scatter.3.cloned.1.call-start = ((), (), s32[]{:S(2)}) async-start(), calls=%async_computation.3 | async-start | bytes 9437184 | tf_op jit(solution)/shard_map/reduce_scatter | solution.py:31
  119.0 1.2 copy-start.3
  124.2 5.2 %copy-start.2 = (f32[32,1024]{1,0:T(8,128)S(1)}, f32[32,1024]{1,0:T(8,128)}, u32[]{:S(2)}) copy-start(f32[32,1024]{1,0:T(8,128)} %get-tuple-element.5) | copy-start | bytes 393220
  124.2 209.6 %copy-start.1 = (bf16[1,1024,1024]{2,1,0:T(8,128)(2,1)S(1)}, bf16[1,1024,1024]{2,1,0:T(8,128)(2,1)}, u32[]{:S(2)}) copy-start(bf16[1,1024,1024]{2,1,0:T(8,128)(2,1)} %param.12) | copy-start | bytes 6291460
  124.2 213.9 %all-to-all-start = ((bf16[8,1024,512]{2,1,0:T(8,128)(2,1)}), bf16[8,1024,512]{2,1,0:T(8,128)(2,1)}, u32[]{:S(2)}, u32[]{:S(2)}) async-start(bf16[8,1024,512]{2,1,0:T(8,128)(2,1)} %stack.3), calls=%async_computation.1 | async-start | bytes 16777216 | tf_op jit(solution)/shard_map/all_to_all | solution.py:22
  130.3 214.8 %copy-start.4 = (f32[4,32,1024]{2,1,0:T(8,128)}, f32[4,32,1024]{2,1,0:T(8,128)S(1)}, u32[]{:S(2)}) copy-start(f32[4,32,1024]{2,1,0:T(8,128)S(1)} %get-tuple-element.8) | copy-start | bytes 1572868
  130.3 214.8 %copy-start.5 = (f32[4,32,1024]{2,1,0:T(8,128)}, f32[4,32,1024]{2,1,0:T(8,128)S(1)}, u32[]{:S(2)}) copy-start(f32[4,32,1024]{2,1,0:T(8,128)S(1)} %get-tuple-element.7) | copy-start | bytes 1572868
Sparse Core Ops, SparseCore 0:
  12.7 93.3 reduce-scatter.4
  109.2 224.5 all-gather.1
Sparse Core Ops, SparseCore 1:
  119.1 281.1 reduce-scatter.2
